TPU v7x, 32 devices: a whole 2x2x4 slice. The times are simulated.
32 devices in a mesh: dp: 1, dap: 32 (over z, y, x, core).
Axes of the slice: x: 2, y: 2, z: 4, core: 2. Of those that a mesh axis runs over, the one named last changes fastest.
Arguments:
- alignment: bfloat16 [128, 256, 256], P(('dp', 'dap')), may hold values from -6 to 6
- pair_rep: bfloat16 [256, 256, 128], P(('dp', 'dap')), may hold values from -6 to 6
- align_mask: int32 [128, 256], P(('dp', 'dap')), may hold values 0 or 1
- residue_mask: int32 [256], P('dp'), may hold values 0 or 1
- row_gain: float32 [256], replicated, may hold values from 0.1 to 1.9
- pair_gain: float32 [128], replicated, may hold values from 0.1 to 1.9
- row_bias: bfloat16 [128, 8], replicated, may hold values from -0.5 to 0.5
- row_scoring: bfloat16 [256, 512], replicated, may hold values from -4 to 4
- row_values: bfloat16 [256, 512], replicated, may hold values from -0.375 to 0.375
- row_output: bfloat16 [256, 256], replicated, may hold values from -0.375 to 0.375
- column_gain: float32 [256], replicated, may hold values from 0.1 to 1.9
- column_scoring: bfloat16 [256, 512], replicated, may hold values from -4 to 4
- column_values: bfloat16 [256, 512], replicated, may hold values from -0.375 to 0.375
- column_output: bfloat16 [256, 256], replicated, may hold values from -0.375 to 0.375
- outer_gain: float32 [256], replicated, may hold values from 0.1 to 1.9
- outer_inputs: bfloat16 [256, 64], replicated, may hold values from -0.375 to 0.375
- outer_output: bfloat16 [1024, 128], replicated, may hold values from -1 to 1
Outputs:
- new_alignment: bfloat16 [128, 256, 256], P(('dp', 'dap'))
- new_pair: bfloat16 [256, 256, 128], P(('dp', 'dap'))
All inputs are finite; a program needn't handle non-finite values. No bound on the sum of `align_mask` on one device may be relied on, other than what follows from the above.
Results may differ from a plain program's by a relative error of at most 0.012.
The roundings to bfloat16 on the way count: a program that leaves them out, or rounds other values in their place, can miss the bound.
Values may be sent and summed in bfloat16 or wider, within the bound.
A program may use at most 64 MiB of HBM per device.

v0:
```python
import math
import jax
import jax.numpy as jnp
from jax import lax
from jax.sharding import PartitionSpec as P

HEADS = 8
HEAD = 32
C_OPM = 32


def layer_norm(values_in, gain):
    wide = values_in.astype(jnp.float32)
    average = jnp.mean(wide, axis=-1, keepdims=True)
    centred = wide - average
    spread = jnp.mean(centred * centred, axis=-1, keepdims=True)
    return (centred * lax.rsqrt(spread + 1e-05) * gain).astype(jnp.bfloat16)


def linear(inputs, weight):
    return jnp.einsum("...c,cd->...d", inputs, weight, preferred_element_type=jnp.float32)


def split_heads(tensor):
    return tensor.reshape(tensor.shape[:2] + (HEADS, HEAD))


def row_attend(queries, keys_all, values_all, gates, keep_mask, bias_term):
    scores = jnp.einsum(
        "sihd,sjhd->shij",
        split_heads(queries),
        split_heads(keys_all),
        preferred_element_type=jnp.float32,
    )
    scores = scores / math.sqrt(HEAD) + bias_term[None]
    scores = jnp.where(keep_mask[:, None, None, :] > 0, scores, -1000000000.0)
    weights = jax.nn.softmax(scores, axis=-1).astype(jnp.bfloat16)
    mixed = jnp.einsum(
        "shij,sjhd->sihd", weights, split_heads(values_all), preferred_element_type=jnp.float32
    )
    mixed = mixed.reshape(queries.shape)
    return (mixed * jax.nn.sigmoid(gates.astype(jnp.float32))).astype(jnp.bfloat16)


def column_attend(queries, keys_all, values_all, gates, keep_mask):
    scores = jnp.einsum(
        "srhd,trhd->rhst",
        split_heads(queries),
        split_heads(keys_all),
        preferred_element_type=jnp.float32,
    )
    scores = scores / math.sqrt(HEAD)
    keep_turned = jnp.swapaxes(keep_mask, 0, 1)
    scores = jnp.where(keep_turned[:, None, None, :] > 0, scores, -1000000000.0)
    weights = jax.nn.softmax(scores, axis=-1).astype(jnp.bfloat16)
    mixed = jnp.einsum(
        "rhst,trhd->srhd", weights, split_heads(values_all), preferred_element_type=jnp.float32
    )
    mixed = mixed.reshape(queries.shape)
    return (mixed * jax.nn.sigmoid(gates.astype(jnp.float32))).astype(jnp.bfloat16)


def body(
    alignment,
    pair_rep,
    align_mask,
    residue_mask,
    row_gain,
    pair_gain,
    row_bias,
    row_scoring,
    row_values,
    row_output,
    column_gain,
    column_scoring,
    column_values,
    column_output,
    outer_gain,
    outer_inputs,
    outer_output,
):
    channels = alignment.shape[2]
    rows_here = pair_rep.shape[0]
    mask_float = align_mask.astype(jnp.float32)
    mask_narrow = align_mask.astype(jnp.bfloat16)
    residue_float = residue_mask.astype(jnp.float32)
    pair_bias = jnp.einsum(
        "ijz,zh->hij", layer_norm(pair_rep, pair_gain), row_bias, preferred_element_type=jnp.float32
    ).astype(jnp.bfloat16)
    normed = layer_norm(alignment, row_gain)
    joint = linear(normed, row_scoring).astype(jnp.bfloat16)
    gated = linear(normed, row_values).astype(jnp.bfloat16)
    queries, keys_all = (joint[..., :channels], joint[..., channels:])
    values_all, gates = (gated[..., :channels], gated[..., channels:])
    keep_rows = mask_float * residue_float[None, :]
    mixed = row_attend(
        queries,
        keys_all,
        values_all,
        gates,
        keep_rows,
        lax.all_gather(pair_bias, "dap", axis=1, tiled=True).astype(jnp.float32),
    )
    row_update = linear(mixed, row_output)
    first_update = (alignment.astype(jnp.float32) + row_update).astype(jnp.bfloat16)
    columns, column_keep = (
        lax.all_to_all(first_update, "dap", split_axis=1, concat_axis=0, tiled=True),
        lax.all_to_all(mask_narrow, "dap", split_axis=1, concat_axis=0, tiled=True),
    )
    keep_columns = column_keep.astype(jnp.float32)
    column_normed = layer_norm(columns, column_gain)
    column_joint = linear(column_normed, column_scoring).astype(jnp.bfloat16)
    column_gated = linear(column_normed, column_values).astype(jnp.bfloat16)
    column_mixed = column_attend(
        column_joint[..., :channels],
        column_joint[..., channels:],
        column_gated[..., :channels],
        column_gated[..., channels:],
        keep_columns,
    )
    second_update = (columns.astype(jnp.float32) + linear(column_mixed, column_output)).astype(
        jnp.bfloat16
    )
    new_alignment = lax.all_to_all(second_update, "dap", split_axis=0, concat_axis=1, tiled=True)
    outer_normed = layer_norm(new_alignment, outer_gain)
    sides = (linear(outer_normed, outer_inputs) * mask_float[..., None]).astype(jnp.bfloat16)
    left_side = lax.all_to_all(sides[..., :C_OPM], "dap", split_axis=1, concat_axis=0, tiled=True)
    right_side, right_keep = (
        lax.all_gather(sides[..., C_OPM:], "dap", axis=0, tiled=True),
        lax.all_gather(mask_narrow, "dap", axis=0, tiled=True),
    )
    pair_count = jnp.dot(
        jnp.swapaxes(column_keep, 0, 1), right_keep, preferred_element_type=jnp.float32
    )
    total_res = right_side.shape[1]
    span = math.gcd(total_res, 128)
    block_count = total_res // span
    right_blocks = jnp.moveaxis(
        right_side.reshape(right_side.shape[0], block_count, span, C_OPM), 1, 0
    )

    def outer_block(right_piece):
        products = jnp.einsum(
            "sic,sje->ijce", left_side, right_piece, preferred_element_type=jnp.float32
        ).astype(jnp.bfloat16)
        flat = products.reshape(rows_here, span, C_OPM * C_OPM)
        return linear(flat, outer_output)

    outer_rows = lax.map(outer_block, right_blocks)
    outer_rows = jnp.moveaxis(outer_rows, 0, 1).reshape(rows_here, total_res, outer_output.shape[1])
    offset = lax.axis_index("dap") * rows_here
    row_factor = lax.dynamic_slice_in_dim(residue_float, offset, rows_here)
    scaled = (
        outer_rows
        / (0.001 + pair_count)[..., None]
        * row_factor[:, None, None]
        * residue_float[None, :, None]
    )
    new_pair = (pair_rep.astype(jnp.float32) + scaled).astype(jnp.bfloat16)
    return (new_alignment, new_pair)


def solution(mesh):
    in_specs = (
        P(("dp", "dap"), None, None),
        P(("dp", "dap"), None, None),
        P(("dp", "dap"), None),
        P("dp"),
        P(),
        P(),
        P(),
        P(),
        P(),
        P(),
        P(),
        P(),
        P(),
        P(),
        P(),
        P(),
        P(),
    )
    out_specs = (P(("dp", "dap"), None, None), P(("dp", "dap"), None, None))
    return jax.shard_map(body, mesh=mesh, in_specs=in_specs, out_specs=out_specs, check_vma=False)
```

profile of v0, /device:TPU:0, one launch (start us, length us, event | category | flops | bytes accessed | tf_op | source)
XLA Modules:
  0.0 223.3 jit_solution(6364969437507721524)
XLA Ops:
  7.2 1.3 convert_reduce_fusion
  8.5 1.7 fusion.27
  10.3 2.5 %fusion.26 = bf16[8,8,256]{2,0,1:T(8,128)(2,1)} fusion(bf16[8,256,128]{2,1,0:T(8,128)(2,1)} %param.20, f32[128]{0:T(128)} %param.24, f32[8,256]{1,0:T(8,128)S(1)} %add_rsqrt_fusion.2, f32[8,256]{1,0:T(8,128)S(1)} %broadcast_multiply_fusion.2, bf16[128,8]{0,1:T(8,128)(2,1)} %param.25), kind=kOutput, calls=%fused_computation.50 | convolution fusion | flops 5521408 | bytes 576000 | tf_op jit(solution)/shard_map/ijz,zh->hij/dot_general | solution.py:87
  12.7 0.8 fusion.72
  13.6 0.6 copy.118
  14.2 7.3 %all-to-all-start.1 = ((bf16[4,32,8]{2,0,1:T(4,128)(2,1)}), bf16[4,32,8]{2,0,1:T(4,128)(2,1)S(1)}, u32[]{:S(2)}, u32[]{:S(2)}) async-start(bf16[4,32,8]{2,0,1:T(4,128)(2,1)} %copy.118), calls=%async_computation.1 | async-start | bytes 65536 | tf_op jit(solution)/shard_map/all_to_all | solution.py:108
  21.5 1.3 convert_reduce_fusion.1
  22.8 1.4 fusion.30
  24.3 1.5 convolution_convert_fusion.2
  25.9 0.2 copy.102
  26.1 1.0 copy.103
  27.1 0.5 convolution_convert_fusion.3
  27.7 1.1 copy.101
  28.8 40.5 %all-gather.4.cloned.1.call-done = bf16[8,256,256]{2,0,1:T(8,128)(2,1)} async-done(((bf16[8,8,256]{2,0,1:T(8,128)(2,1)}), bf16[8,256,256]{2,0,1:T(8,128)(2,1)}) %all-gather.4.cloned.1.call-update) | async-done | bytes 1048592 | tf_op jit(solution)/shard_map/all_gather | solution.py:102
  69.3 1.9 copy.104
  71.1 7.6 %fusion.73 = (f32[4,8,256]{2,1,0:T(8,128)S(1)}, f32[4,8,256,256]{2,3,1,0:T(8,128)}) fusion(f32[8,256,256]{1,2,0:T(8,128)S(1)} %copy.104, pred[4,256]{1,0:T(4,128)(4,1)S(1)} %multiply_compare_fusion, bf16[4,256,8,32]{1,3,2,0:T(8,128)(2,1)S(1)} %bitcast.152, bf16[4,256,8,32]{1,3,2,0:T(8,128)(2,1)} %bitcast.153), kind=kOutput, calls=%fused_computation.113 | convolution fusion | flops 144703744 | bytes 11568128 | tf_op jit(solution)/shard_map/sub | solution.py:37
  78.8 4.4 %fusion.13 = f32[4,8,32,256]{3,2,1,0:T(8,128)S(1)} fusion(bf16[4,256,8,32]{1,3,2,0:T(8,128)(2,1)} %bitcast.154, f32[4,8,256,256]{2,3,1,0:T(8,128)} %get-tuple-element.64, f32[4,8,256]{2,1,0:T(8,128)S(1)} %get-tuple-element.63), kind=kOutput, calls=%fused_computation.21 | convolution fusion | flops 138412032 | bytes 9994240 | tf_op jit(solution)/shard_map/shij,sjhd->sihd/dot_general | solution.py:38
  83.2 0.3 copy.106
  83.6 1.5 fusion.19
  85.0 1.2 copy.107
  86.2 3.6 %all-to-all-start = ((bf16[4,256,256]{2,0,1:T(4,128)(2,1)}), bf16[4,256,256]{2,0,1:T(4,128)(2,1)S(1)}, u32[]{:S(2)}, u32[]{:S(2)}) async-start(bf16[4,256,256]{2,0,1:T(4,128)(2,1)} %copy.107), calls=%async_computation | async-start | bytes 1048576 | tf_op jit(solution)/shard_map/all_to_all | solution.py:107
  89.8 0.2 all-gather.6.cloned.1.call-start
  90.1 15.2 %all-to-all-done = bf16[4,256,256]{2,0,1:T(4,128)(2,1)S(1)} async-done(((bf16[4,256,256]{2,0,1:T(4,128)(2,1)}), bf16[4,256,256]{2,0,1:T(4,128)(2,1)S(1)}, u32[]{:S(2)}, u32[]{:S(2)}) %all-to-all-start) | async-done | bytes 524320 | tf_op jit(solution)/shard_map/all_to_all | solution.py:107
  105.5 0.2 fusion.68
  105.8 0.2 copy.156
  106.2 0.4 multiply_reduce_fusion
  106.9 0.7 copy.109
  107.6 0.4 reshape.156
  108.0 0.5 convolution_convert_fusion
  108.7 0.3 copy.120
  108.9 1.0 copy.121
  109.9 0.5 convolution_convert_fusion.1
  110.5 1.0 copy.117
  111.5 4.8 %fusion.74 = (f32[8,8,128]{2,1,0:T(8,128)S(1)}, f32[8,8,128,128]{2,3,1,0:T(8,128)}) fusion(pred[8,128]{1,0:T(8,128)(4,1)S(1)} %copy.119, bf16[128,8,8,32]{0,3,2,1:T(8,128)(2,1)S(1)} %bitcast.155, bf16[128,8,8,32]{0,3,2,1:T(8,128)(2,1)} %bitcast.156), kind=kOutput, calls=%fused_computation.114 | convolution fusion | flops 71303296 | bytes 5276672 | tf_op jit(solution)/shard_map/sub | solution.py:55
  116.3 3.0 %fusion.17 = f32[8,8,32,128]{3,2,1,0:T(8,128)S(1)} fusion(bf16[128,8,8,32]{0,3,2,1:T(8,128)(2,1)} %bitcast.157, f32[8,8,128,128]{2,3,1,0:T(8,128)} %get-tuple-element.66, f32[8,8,128]{2,1,0:T(8,128)S(1)} %get-tuple-element.65), kind=kOutput, calls=%fused_computation.26 | convolution fusion | flops 69206016 | bytes 5799936 | tf_op jit(solution)/shard_map/rhst,trhd->srhd/dot_general | solution.py:56
  119.4 1.3 copy.123
  120.7 1.7 fusion.20
  122.4 0.3 copy.124
  122.7 18.4 %all_to_all.64 = bf16[128,8,256]{2,1,0:T(8,128)(2,1)S(1)} all-to-all(bf16[128,8,256]{2,1,0:T(8,128)(2,1)S(1)} %copy.124), channel_id=1, replica_groups=mesh['dp'=1,'dap'=32] {'dap'}, dimensions={0} | all-to-all | bytes 1048576 | tf_op jit(solution)/shard_map/all_to_all | solution.py:124
  141.1 0.4 convert_reduce_fusion.2
  141.4 0.2 copy.158
  142.0 0.7 fusion.34
  143.0 0.3 copy.157
  143.4 0.5 fusion.25
  143.9 0.6 fusion.71
  144.7 39.2 %all-gather = bf16[32,4,256]{2,1,0:T(4,128)(2,1)S(1)} all-gather(bf16[1,4,256]{2,1,0:T(4,128)(2,1)S(1)} %bitcast.162), channel_id=1, replica_groups=mesh['dp'=1,'dap'=32] {'dap'}, dimensions={0}, use_global_device_ids=true | all-gather | bytes 67584 | tf_op jit(solution)/shard_map/all_gather | solution.py:130
  183.9 0.2 copy.133
  184.1 0.8 reshape.172
  185.0 2.8 %all-to-all-start.3 = ((bf16[32,2,512]{2,1,0:T(2,128)(2,1)}), bf16[32,2,512]{2,1,0:T(2,128)(2,1)S(1)}, u32[]{:S(2)}, u32[]{:S(2)}) async-start(bf16[32,2,512]{2,1,0:T(2,128)(2,1)} %reshape.172), calls=%async_computation.3 | async-start | bytes 131072 | tf_op jit(solution)/shard_map/all_to_all | solution.py:127
  187.9 7.5 %all-to-all-done.3 = bf16[32,2,512]{2,1,0:T(2,128)(2,1)S(1)} async-done(((bf16[32,2,512]{2,1,0:T(2,128)(2,1)}), bf16[32,2,512]{2,1,0:T(2,128)(2,1)S(1)}, u32[]{:S(2)}, u32[]{:S(2)}) %all-to-all-start.3) | async-done | bytes 65568 | tf_op jit(solution)/shard_map/all_to_all | solution.py:127
  195.4 0.2 reshape.173
  195.7 0.2 copy.136
  195.9 3.8 %all-gather.6.cloned.1.call-done = bf16[128,256,32]{1,2,0:T(8,128)(2,1)} async-done(((bf16[4,256,32]{1,2,0:T(8,128)(2,1)}), bf16[128,256,32]{1,2,0:T(8,128)(2,1)}) %all-gather.6.cloned.1.call-update) | async-done | bytes 2097168 | tf_op jit(solution)/shard_map/all_gather | solution.py:129
  199.7 4.0 %reshape.154 = bf16[128,2,128,32]{2,1,3,0:T(2,128)(2,1)} reshape(bf16[128,256,32]{1,2,0:T(8,128)(2,1)} %all-gather.6.cloned.1.call-done) | data formatting | bytes 4194304 | tf_op jit(solution)/shard_map/reshape | solution.py:139
  203.7 2.9 %copy.155 = bf16[128,2,128,32]{2,0,3,1:T(8,128)(2,1)S(1)} copy(bf16[128,2,128,32]{2,1,3,0:T(2,128)(2,1)} %reshape.154) | data formatting | bytes 4194304 | tf_op jit(solution)/shard_map/reshape | solution.py:139
  206.6 7.3 %while.10 = (s32[]{:T(128)}, f32[2,8,128,128]{3,2,1,0:T(8,128)}, bf16[2,128,128,32]{2,1,3,0:T(8,128)(2,1)S(1)}, bf16[128,8,32]{0,2,1:T(8,128)(2,1)S(1)}, bf16[1024,128]{1,0:T(8,128)(2,1)S(1)}, /*index=5*/s32[]{:T(128)}) while((s32[]{:T(128)}, f32[2,8,128,128]{3,2,1,0:T(8,128)}, bf16[2,128,128,32]{2,1,3,0:T(8,128)(2,1)S(1)}, ...), condition=%wide.region_13.14_spmd, body=%wide.region_12.13_spmd.sunk | while | flops 537919488 | bytes 10289737 | solution.py:149
  206.6 0.7 convert_bitcast_fusion.2
  207.3 1.4 copy.161
  208.7 1.6 fusion.97
  210.3 0.7 convert_bitcast_fusion.2
  211.0 1.4 copy.161
  212.3 1.6 fusion.97
  213.9 1.3 copy.137
  215.2 1.2 fusion.35
  (74 shorter events, 2.4 us)
Async XLA Ops:
  7.2 17.1 %copy-start = (bf16[256,512]{1,0:T(8,128)(2,1)S(1)}, bf16[256,512]{1,0:T(8,128)(2,1)}, u32[]{:S(2)}) copy-start(bf16[256,512]{1,0:T(8,128)(2,1)} %param.26) | copy-start | bytes 786436
  7.2 62.1 %all-gather.4.cloned.1.call-start = ((), (), s32[]{:S(2)}) async-start(), calls=%async_computation.4 | async-start | bytes 1081344 | tf_op jit(solution)/shard_map/all_gather | solution.py:102
  10.2 16.9 %copy-start.10 = (s32[256]{0:T(256)S(1)}, s32[256]{0:T(256)}, u32[]{:S(2)}) copy-start(s32[256]{0:T(256)} %param.22) | copy-start | bytes 3076
  10.2 16.9 %copy-start.3 = (bf16[4,256,256]{2,1,0:T(8,128)(2,1)S(1)}, bf16[4,256,256]{2,1,0:T(8,128)(2,1)}, u32[]{:S(2)}) copy-start(bf16[4,256,256]{2,1,0:T(8,128)(2,1)} %param.19) | copy-start | bytes 1572868
  10.2 16.9 %copy-start.11 = (bf16[256,512]{1,0:T(8,128)(2,1)S(1)}, bf16[256,512]{1,0:T(8,128)(2,1)}, u32[]{:S(2)}) copy-start(bf16[256,512]{1,0:T(8,128)(2,1)} %param.27) | copy-start | bytes 786436
  10.3 16.9 %copy-start.14 = (f32[256]{0:T(256)S(1)}, f32[256]{0:T(256)}, u32[]{:S(2)}) copy-start(f32[256]{0:T(256)} %param.23) | copy-start | bytes 3076
  14.2 72.0 %all-to-all-start.1 = ((bf16[4,32,8]{2,0,1:T(4,128)(2,1)}), bf16[4,32,8]{2,0,1:T(4,128)(2,1)S(1)}, u32[]{:S(2)}, u32[]{:S(2)}) async-start(bf16[4,32,8]{2,0,1:T(4,128)(2,1)} %copy.118), calls=%async_computation.1 | async-start | bytes 65536 | tf_op jit(solution)/shard_map/all_to_all | solution.py:108
  25.8 3.0 %copy-start.8 = (s32[4,256]{1,0:T(4,128)S(1)}, s32[4,256]{1,0:T(4,128)}, u32[]{:S(2)}) copy-start(s32[4,256]{1,0:T(4,128)} %param.21) | copy-start | bytes 12292
  27.6 1.2 copy-start.7
  78.8 4.8 %copy-start.12 = (bf16[256,256]{1,0:T(8,128)(2,1)S(1)}, bf16[256,256]{1,0:T(8,128)(2,1)}, u32[]{:S(2)}) copy-start(bf16[256,256]{1,0:T(8,128)(2,1)} %param.28) | copy-start | bytes 393220
  86.2 19.1 %all-to-all-start = ((bf16[4,256,256]{2,0,1:T(4,128)(2,1)}), bf16[4,256,256]{2,0,1:T(4,128)(2,1)S(1)}, u32[]{:S(2)}, u32[]{:S(2)}) async-start(bf16[4,256,256]{2,0,1:T(4,128)(2,1)} %copy.107), calls=%async_computation | async-start | bytes 1048576 | tf_op jit(solution)/shard_map/all_to_all | solution.py:107
  89.8 109.9 %all-gather.6.cloned.1.call-start = ((), (), s32[]{:S(2)}) async-start(), calls=%async_computation.5 | async-start | bytes 2162688 | tf_op jit(solution)/shard_map/all_gather | solution.py:129
  105.7 2.3 %copy-start.5 = (bf16[256,512]{1,0:T(8,128)(2,1)S(1)}, bf16[256,512]{1,0:T(8,128)(2,1)}, u32[]{:S(2)}) copy-start(bf16[256,512]{1,0:T(8,128)(2,1)} %param.30) | copy-start | bytes 786436
  105.7 2.3 %copy-start.9 = (f32[256]{0:T(256)S(1)}, f32[256]{0:T(256)}, u32[]{:S(2)}) copy-start(f32[256]{0:T(256)} %param.29) | copy-start | bytes 3076
  107.6 2.4 %copy-start.6 = (bf16[256,512]{1,0:T(8,128)(2,1)S(1)}, bf16[256,512]{1,0:T(8,128)(2,1)}, u32[]{:S(2)}) copy-start(bf16[256,512]{1,0:T(8,128)(2,1)} %param.31) | copy-start | bytes 786436
  122.3 21.1 %copy-start.13 = (bf16[256,64]{0,1:T(8,128)(2,1)S(1)}, bf16[256,64]{0,1:T(8,128)(2,1)}, u32[]{:S(2)}) copy-start(bf16[256,64]{0,1:T(8,128)(2,1)} %param.34) | copy-start | bytes 98308
  122.3 21.1 %copy-start.15 = (f32[256]{0:T(256)S(1)}, f32[256]{0:T(256)}, u32[]{:S(2)}) copy-start(f32[256]{0:T(256)} %param.33) | copy-start | bytes 3076
  143.3 52.4 %copy-start.4 = (bf16[4,32,8,256]{3,2,1,0:T(8,128)(2,1)}, bf16[4,32,8,256]{3,2,1,0:T(8,128)(2,1)S(1)}, u32[]{:S(2)}) copy-start(bf16[4,32,8,256]{3,2,1,0:T(8,128)(2,1)S(1)} %copy.157) | copy-start | bytes 1572868
  185.0 10.4 %all-to-all-start.3 = ((bf16[32,2,512]{2,1,0:T(2,128)(2,1)}), bf16[32,2,512]{2,1,0:T(2,128)(2,1)S(1)}, u32[]{:S(2)}, u32[]{:S(2)}) async-start(bf16[32,2,512]{2,1,0:T(2,128)(2,1)} %reshape.172), calls=%async_computation.3 | async-start | bytes 131072 | tf_op jit(solution)/shard_map/all_to_all | solution.py:127
  195.9 10.7 %copy-start.1 = (bf16[1024,128]{1,0:T(8,128)(2,1)S(1)}, bf16[1024,128]{1,0:T(8,128)(2,1)}, u32[]{:S(2)}) copy-start(bf16[1024,128]{1,0:T(8,128)(2,1)} %param.35) | copy-start | bytes 786436
  206.6 8.6 %copy-start.2 = (bf16[8,256,128]{2,1,0:T(8,128)(2,1)S(1)}, bf16[8,256,128]{2,1,0:T(8,128)(2,1)}, u32[]{:S(2)}) copy-start(bf16[8,256,128]{2,1,0:T(8,128)(2,1)} %param.20) | copy-start | bytes 1572868
Sparse Core Ops, SparseCore 0:
  12.9 56.3 all-gather.3
  144.7 54.9 all-gather.5
where the time goes:
time: 224 us; the launch traced here: 223 us
  waiting for transfers between devices  67 us (30%)
  blocking collectives  57.6 us (26%)
  matrix products  33.7 us (15%)
  local copies, waits for them, and re-layouts  26.9 us (12%)
  between operations  14.6 us (7%)
  starting transfers between devices  13.9 us (6%)
  other arithmetic  9.53 us (4%)
    all_gather x1, waiting for transfers between devices, body(): lax.all_gather(pair_bias, 'dap', axis=1, tiled=True).astype(jnp.float32)  40.5 us
    all_gather x1, blocking collectives, body(): lax.all_gather(mask_narrow, 'dap', axis=0, tiled=True)  39.2 us
    all_to_all x1, blocking collectives, body(): lax.all_to_all(second_update, 'dap', split_axis=0, concat_axis=1, tiled=T...  18.4 us
    all_to_all x1, waiting for transfers between devices, body(): lax.all_to_all(first_update, 'dap', split_axis=1, concat_axis=0, tiled=True)  15.2 us
    dot_general x9, matrix products, linear(): jnp.einsum('...c,cd->...d', inputs, weight, preferred_element_type=jnp.fl...  9.78 us
    sub x1, matrix products, row_attend(): weights = jax.nn.softmax(scores, axis=-1).astype(jnp.bfloat16)  7.63 us
    all_to_all x1, waiting for transfers between devices, body(): lax.all_to_all(sides[..., :C_OPM], 'dap', split_axis=1, concat_axis=0, ti...  7.48 us
    all_to_all x1, starting transfers between devices, body(): lax.all_to_all(mask_narrow, 'dap', split_axis=1, concat_axis=0, tiled=True)  7.3 us
  transfers between devices with their start and end apart: 5, of which 4 were waited for; matrix products, arithmetic and copies ran while one was open for 12% of the time, Pallas kernels for 0%

commit v1 on v0

--- a/solution.py
+++ b/solution.py
@@ -124,7 +124,12 @@
     new_alignment = lax.all_to_all(second_update, "dap", split_axis=0, concat_axis=1, tiled=True)
     outer_normed = layer_norm(new_alignment, outer_gain)
     sides = (linear(outer_normed, outer_inputs) * mask_float[..., None]).astype(jnp.bfloat16)
-    left_side = lax.all_to_all(sides[..., :C_OPM], "dap", split_axis=1, concat_axis=0, tiled=True)
+    left_side = jnp.concatenate(
+        lax.all_to_all(
+            jnp.stack(jnp.split(sides[..., :C_OPM], lax.axis_size("dap"), axis=1)), "dap", 0, 0
+        ),
+        axis=0,
+    )
     right_side, right_keep = (
         lax.all_gather(sides[..., C_OPM:], "dap", axis=0, tiled=True),
         lax.all_gather(mask_narrow, "dap", axis=0, tiled=True),

time: 224 us -> 253 us (1.13)
  waiting for transfers between devices: 67 us -> 102 us
  blocking collectives: 57.6 us -> 43.8 us
  local copies, waits for them, and re-layouts: 26.9 us -> 30.8 us
  starting transfers between devices: 13.9 us -> 17 us
    all_gather x1, waiting for transfers between devices: 3.78 us -> 39.3 us  [body(): lax.all_gather(sides[..., C_OPM:], 'dap', axis=0, tiled=True)]
    all_to_all x1 -> x0, blocking collectives: 18.4 us -> none  [body(): lax.all_to_all(second_update, 'dap', split_axis=0, concat_axis=1, tiled=T...]
    all_gather x1, blocking collectives: 39.2 us -> 43.8 us  [body(): lax.all_gather(mask_narrow, 'dap', axis=0, tiled=True)]
    another operation x0 -> x35, local copies, waits for them, and re-layouts: none -> 3.13 us  [body(): jnp.stack(jnp.split(sides[..., :C_OPM], lax.axis_size('dap'), axis=1))]
    all_to_all x1 -> x2, starting transfers between devices: 2.79 us -> 5.86 us  [the longest x1 3.08 us: body(): lax.all_to_all(second_update, 'dap', split_axis=0, concat_axis=1, tiled=T...]
    all_to_all x1 -> x2, waiting for transfers between devices: 7.48 us -> 7.06 us  [the longest x1 7.06 us: body(): lax.all_to_all(jnp.stack(jnp.split(sides[..., :C_OPM], lax.axis_size('dap...]
  transfers between devices with their start and end apart: 5 -> 6, of which waited for: 4 -> 4; matrix products, arithmetic and copies ran while one was open for 12% -> 12% of each run, Pallas kernels for 0% -> 0%
where the time goes in v1:
time: 253 us; the launch traced here: 252 us
  waiting for transfers between devices  102 us (40%)
  blocking collectives  43.8 us (17%)
  matrix products  33.7 us (13%)
  local copies, waits for them, and re-layouts  30.8 us (12%)
  starting transfers between devices  17 us (7%)
  between operations  14.7 us (6%)
  other arithmetic  9.53 us (4%)
    all_gather x1, blocking collectives, body(): lax.all_gather(mask_narrow, 'dap', axis=0, tiled=True)  43.8 us
    all_gather x1, waiting for transfers between devices, body(): lax.all_gather(pair_bias, 'dap', axis=1, tiled=True).astype(jnp.float32)  40.5 us
    all_gather x1, waiting for transfers between devices, body(): lax.all_gather(sides[..., C_OPM:], 'dap', axis=0, tiled=True)  39.3 us
    all_to_all x1, waiting for transfers between devices, body(): lax.all_to_all(first_update, 'dap', split_axis=1, concat_axis=0, tiled=True)  15.3 us
    dot_general x9, matrix products, linear(): jnp.einsum('...c,cd->...d', inputs, weight, preferred_element_type=jnp.fl...  9.77 us
    sub x1, matrix products, row_attend(): weights = jax.nn.softmax(scores, axis=-1).astype(jnp.bfloat16)  7.63 us
    all_to_all x1, starting transfers between devices, body(): lax.all_to_all(mask_narrow, 'dap', split_axis=1, concat_axis=0, tiled=True)  7.3 us
    all_to_all x1, waiting for transfers between devices, body(): lax.all_to_all(jnp.stack(jnp.split(sides[..., :C_OPM], lax.axis_size('dap...  7.06 us
  transfers between devices with their start and end apart: 6, of which 4 were waited for; matrix products, arithmetic and copies ran while one was open for 12% of the time, Pallas kernels for 0%

profile of v1, /device:TPU:0, one launch (start us, length us, event | category | flops | bytes accessed | tf_op | source)
XLA Modules:
  0.0 251.7 jit_solution(14338894560495986353)
XLA Ops:
  7.2 1.3 convert_reduce_fusion
  8.5 1.7 fusion.27
  10.3 2.5 fusion.26
  12.8 0.8 fusion.71
  13.6 0.6 copy.145
  14.3 7.3 %all-to-all-start.1 = ((bf16[4,32,8]{2,0,1:T(4,128)(2,1)}), bf16[4,32,8]{2,0,1:T(4,128)(2,1)S(1)}, u32[]{:S(2)}, u32[]{:S(2)}) async-start(bf16[4,32,8]{2,0,1:T(4,128)(2,1)} %copy.145), calls=%async_computation.1 | async-start | bytes 65536 | tf_op jit(solution)/shard_map/all_to_all | solution.py:108
  21.6 1.3 convert_reduce_fusion.1
  22.9 1.4 fusion.30
  24.3 1.5 convolution_convert_fusion.2
  25.9 0.2 copy.129
  26.1 1.0 copy.130
  27.2 0.5 convolution_convert_fusion.3
  27.7 1.1 copy.128
  28.8 40.5 %all-gather.4.cloned.1.call-done = bf16[8,256,256]{2,0,1:T(8,128)(2,1)} async-done(((bf16[8,8,256]{2,0,1:T(8,128)(2,1)}), bf16[8,256,256]{2,0,1:T(8,128)(2,1)}) %all-gather.4.cloned.1.call-update) | async-done | bytes 1048592 | tf_op jit(solution)/shard_map/all_gather | solution.py:102
  69.3 1.9 copy.131
  71.2 7.6 %fusion.72 = (f32[4,8,256]{2,1,0:T(8,128)S(1)}, f32[4,8,256,256]{2,3,1,0:T(8,128)}) fusion(f32[8,256,256]{1,2,0:T(8,128)S(1)} %copy.131, pred[4,256]{1,0:T(4,128)(4,1)S(1)} %multiply_compare_fusion, bf16[4,256,8,32]{1,3,2,0:T(8,128)(2,1)S(1)} %bitcast.206, bf16[4,256,8,32]{1,3,2,0:T(8,128)(2,1)} %bitcast.207), kind=kOutput, calls=%fused_computation.175 | convolution fusion | flops 144703744 | bytes 11568128 | tf_op jit(solution)/shard_map/sub | solution.py:37
  78.8 4.4 %fusion.13 = f32[4,8,32,256]{3,2,1,0:T(8,128)S(1)} fusion(bf16[4,256,8,32]{1,3,2,0:T(8,128)(2,1)} %bitcast.208, f32[4,8,256,256]{2,3,1,0:T(8,128)} %get-tuple-element.99, f32[4,8,256]{2,1,0:T(8,128)S(1)} %get-tuple-element.98), kind=kOutput, calls=%fused_computation.21 | convolution fusion | flops 138412032 | bytes 9994240 | tf_op jit(solution)/shard_map/shij,sjhd->sihd/dot_general | solution.py:38
  83.2 0.3 copy.133
  83.6 1.5 fusion.19
  85.1 1.2 copy.134
  86.3 3.7 %all-to-all-start = ((bf16[4,256,256]{2,0,1:T(4,128)(2,1)}), bf16[4,256,256]{2,0,1:T(4,128)(2,1)S(1)}, u32[]{:S(2)}, u32[]{:S(2)}) async-start(bf16[4,256,256]{2,0,1:T(4,128)(2,1)} %copy.134), calls=%async_computation | async-start | bytes 1048576 | tf_op jit(solution)/shard_map/all_to_all | solution.py:107
  90.1 15.3 %all-to-all-done = bf16[4,256,256]{2,0,1:T(4,128)(2,1)S(1)} async-done(((bf16[4,256,256]{2,0,1:T(4,128)(2,1)}), bf16[4,256,256]{2,0,1:T(4,128)(2,1)S(1)}, u32[]{:S(2)}, u32[]{:S(2)}) %all-to-all-start) | async-done | bytes 524320 | tf_op jit(solution)/shard_map/all_to_all | solution.py:107
  105.5 0.2 fusion.68
  105.8 0.2 copy.211
  106.3 0.4 multiply_reduce_fusion
  106.9 0.7 copy.136
  107.6 0.4 reshape.160
  108.0 0.5 convolution_convert_fusion
  108.7 0.3 copy.147
  109.0 1.0 copy.148
  110.0 0.5 convolution_convert_fusion.1
  110.5 1.0 copy.144
  111.5 4.8 %fusion.73 = (f32[8,8,128]{2,1,0:T(8,128)S(1)}, f32[8,8,128,128]{2,3,1,0:T(8,128)}) fusion(pred[8,128]{1,0:T(8,128)(4,1)S(1)} %copy.146, bf16[128,8,8,32]{0,3,2,1:T(8,128)(2,1)S(1)} %bitcast.209, bf16[128,8,8,32]{0,3,2,1:T(8,128)(2,1)} %bitcast.210), kind=kOutput, calls=%fused_computation.176 | convolution fusion | flops 71303296 | bytes 5276672 | tf_op jit(solution)/shard_map/sub | solution.py:55
  116.3 3.0 %fusion.17 = f32[8,8,32,128]{3,2,1,0:T(8,128)S(1)} fusion(bf16[128,8,8,32]{0,3,2,1:T(8,128)(2,1)} %bitcast.211, f32[8,8,128,128]{2,3,1,0:T(8,128)} %get-tuple-element.101, f32[8,8,128]{2,1,0:T(8,128)S(1)} %get-tuple-element.100), kind=kOutput, calls=%fused_computation.26 | convolution fusion | flops 69206016 | bytes 5799936 | tf_op jit(solution)/shard_map/rhst,trhd->srhd/dot_general | solution.py:56
  119.4 1.3 copy.150
  120.7 1.7 fusion.20
  122.4 1.1 copy.151
  123.5 3.1 %all-to-all-start.2 = ((bf16[128,8,256]{2,1,0:T(8,128)(2,1)}), bf16[128,8,256]{2,1,0:T(8,128)(2,1)S(1)}, u32[]{:S(2)}, u32[]{:S(2)}) async-start(bf16[128,8,256]{2,1,0:T(8,128)(2,1)} %copy.151), calls=%async_computation.2 | async-start | bytes 1048576 | tf_op jit(solution)/shard_map/all_to_all | solution.py:124
  126.7 43.8 %all-gather = bf16[32,4,256]{2,1,0:T(4,128)(2,1)S(1)} all-gather(bf16[1,4,256]{2,1,0:T(4,128)(2,1)S(1)} %bitcast.216), channel_id=1, replica_groups=mesh['dp'=1,'dap'=32] {'dap'}, dimensions={0}, use_global_device_ids=true | all-gather | bytes 67584 | tf_op jit(solution)/shard_map/all_gather | solution.py:135
  170.6 0.4 convert_reduce_fusion.2
  170.9 0.2 copy.213
  171.5 0.7 fusion.34
  172.5 0.3 copy.212
  172.9 0.5 fusion.25
  173.4 0.6 slice.77
  174.1 0.2 slice_bitcast_fusion.19
  175.3 0.2 slice_bitcast_fusion
  177.6 0.9 reshape.176
  178.4 2.8 %all-to-all-start.3 = ((bf16[32,2,512]{2,1,0:T(2,128)(2,1)}), bf16[32,2,512]{2,1,0:T(2,128)(2,1)S(1)}, u32[]{:S(2)}, u32[]{:S(2)}) async-start(bf16[32,2,512]{2,1,0:T(2,128)(2,1)} %reshape.176), calls=%async_computation.3 | async-start | bytes 131072 | tf_op jit(solution)/shard_map/all_to_all | solution.py:128
  181.4 7.1 %all-to-all-done.3 = bf16[32,2,512]{2,1,0:T(2,128)(2,1)S(1)} async-done(((bf16[32,2,512]{2,1,0:T(2,128)(2,1)}), bf16[32,2,512]{2,1,0:T(2,128)(2,1)S(1)}, u32[]{:S(2)}, u32[]{:S(2)}) %all-to-all-start.3) | async-done | bytes 65568 | tf_op jit(solution)/shard_map/all_to_all | solution.py:128
  188.5 0.2 reshape.177
  188.6 0.2 copy.192
  188.8 39.3 %all-gather.6.cloned.1.call-done = bf16[128,256,32]{1,2,0:T(8,128)(2,1)} async-done(((bf16[4,256,32]{1,2,0:T(8,128)(2,1)}), bf16[128,256,32]{1,2,0:T(8,128)(2,1)}) %all-gather.6.cloned.1.call-update) | async-done | bytes 2097168 | tf_op jit(solution)/shard_map/all_gather | solution.py:134
  228.2 4.0 %reshape.157 = bf16[128,2,128,32]{2,1,3,0:T(2,128)(2,1)} reshape(bf16[128,256,32]{1,2,0:T(8,128)(2,1)} %all-gather.6.cloned.1.call-done) | data formatting | bytes 4194304 | tf_op jit(solution)/shard_map/reshape | solution.py:144
  232.1 2.9 %copy.210 = bf16[128,2,128,32]{2,0,3,1:T(8,128)(2,1)S(1)} copy(bf16[128,2,128,32]{2,1,3,0:T(2,128)(2,1)} %reshape.157) | data formatting | bytes 4194304 | tf_op jit(solution)/shard_map/reshape | solution.py:144
  235.1 7.3 %while.10 = (s32[]{:T(128)}, f32[2,8,128,128]{3,2,1,0:T(8,128)}, bf16[2,128,128,32]{2,1,3,0:T(8,128)(2,1)S(1)}, bf16[128,8,32]{0,2,1:T(8,128)(2,1)S(1)}, bf16[1024,128]{1,0:T(8,128)(2,1)S(1)}, /*index=5*/s32[]{:T(128)}) while((s32[]{:T(128)}, f32[2,8,128,128]{3,2,1,0:T(8,128)}, bf16[2,128,128,32]{2,1,3,0:T(8,128)(2,1)S(1)}, ...), condition=%wide.region_13.14_spmd, body=%wide.region_12.13_spmd.sunk | while | flops 537919488 | bytes 10289737 | solution.py:154
  235.1 0.7 convert_bitcast_fusion.2
  235.8 1.4 copy.215
  237.1 1.6 fusion.96
  238.7 0.7 convert_bitcast_fusion.2
  239.4 1.4 copy.215
  240.8 1.6 fusion.96
  242.3 1.3 copy.193
  243.7 1.2 fusion.35
  (138 shorter events, 5.3 us)
Async XLA Ops:
  7.2 17.1 %copy-start = (bf16[256,512]{1,0:T(8,128)(2,1)S(1)}, bf16[256,512]{1,0:T(8,128)(2,1)}, u32[]{:S(2)}) copy-start(bf16[256,512]{1,0:T(8,128)(2,1)} %param.26) | copy-start | bytes 786436
  7.2 62.1 %all-gather.4.cloned.1.call-start = ((), (), s32[]{:S(2)}) async-start(), calls=%async_computation.4 | async-start | bytes 1081344 | tf_op jit(solution)/shard_map/all_gather | solution.py:102
  10.2 16.9 %copy-start.10 = (s32[256]{0:T(256)S(1)}, s32[256]{0:T(256)}, u32[]{:S(2)}) copy-start(s32[256]{0:T(256)} %param.22) | copy-start | bytes 3076
  10.2 16.9 %copy-start.3 = (bf16[4,256,256]{2,1,0:T(8,128)(2,1)S(1)}, bf16[4,256,256]{2,1,0:T(8,128)(2,1)}, u32[]{:S(2)}) copy-start(bf16[4,256,256]{2,1,0:T(8,128)(2,1)} %param.19) | copy-start | bytes 1572868
  10.2 16.9 %copy-start.11 = (bf16[256,512]{1,0:T(8,128)(2,1)S(1)}, bf16[256,512]{1,0:T(8,128)(2,1)}, u32[]{:S(2)}) copy-start(bf16[256,512]{1,0:T(8,128)(2,1)} %param.27) | copy-start | bytes 786436
  10.3 16.9 %copy-start.14 = (f32[256]{0:T(256)S(1)}, f32[256]{0:T(256)}, u32[]{:S(2)}) copy-start(f32[256]{0:T(256)} %param.23) | copy-start | bytes 3076
  14.3 72.0 %all-to-all-start.1 = ((bf16[4,32,8]{2,0,1:T(4,128)(2,1)}), bf16[4,32,8]{2,0,1:T(4,128)(2,1)S(1)}, u32[]{:S(2)}, u32[]{:S(2)}) async-start(bf16[4,32,8]{2,0,1:T(4,128)(2,1)} %copy.145), calls=%async_computation.1 | async-start | bytes 65536 | tf_op jit(solution)/shard_map/all_to_all | solution.py:108
  25.8 3.0 %copy-start.8 = (s32[4,256]{1,0:T(4,128)S(1)}, s32[4,256]{1,0:T(4,128)}, u32[]{:S(2)}) copy-start(s32[4,256]{1,0:T(4,128)} %param.21) | copy-start | bytes 12292
  27.7 1.2 copy-start.7
  78.8 4.8 %copy-start.12 = (bf16[256,256]{1,0:T(8,128)(2,1)S(1)}, bf16[256,256]{1,0:T(8,128)(2,1)}, u32[]{:S(2)}) copy-start(bf16[256,256]{1,0:T(8,128)(2,1)} %param.28) | copy-start | bytes 393220
  86.3 19.1 %all-to-all-start = ((bf16[4,256,256]{2,0,1:T(4,128)(2,1)}), bf16[4,256,256]{2,0,1:T(4,128)(2,1)S(1)}, u32[]{:S(2)}, u32[]{:S(2)}) async-start(bf16[4,256,256]{2,0,1:T(4,128)(2,1)} %copy.134), calls=%async_computation | async-start | bytes 1048576 | tf_op jit(solution)/shard_map/all_to_all | solution.py:107
  105.8 2.3 copy-start.5
  105.8 2.3 copy-start.9
  107.6 2.4 copy-start.6
  122.3 50.5 %copy-start.13 = (bf16[256,64]{0,1:T(8,128)(2,1)S(1)}, bf16[256,64]{0,1:T(8,128)(2,1)}, u32[]{:S(2)}) copy-start(bf16[256,64]{0,1:T(8,128)(2,1)} %param.34) | copy-start | bytes 98308
  122.4 50.5 %copy-start.15 = (f32[256]{0:T(256)S(1)}, f32[256]{0:T(256)}, u32[]{:S(2)}) copy-start(f32[256]{0:T(256)} %param.33) | copy-start | bytes 3076
  123.5 47.1 %all-to-all-start.2 = ((bf16[128,8,256]{2,1,0:T(8,128)(2,1)}), bf16[128,8,256]{2,1,0:T(8,128)(2,1)S(1)}, u32[]{:S(2)}, u32[]{:S(2)}) async-start(bf16[128,8,256]{2,1,0:T(8,128)(2,1)} %copy.151), calls=%async_computation.2 | async-start | bytes 1048576 | tf_op jit(solution)/shard_map/all_to_all | solution.py:124
  126.5 101.6 %all-gather.6.cloned.1.call-start = ((), (), s32[]{:S(2)}) async-start(), calls=%async_computation.5 | async-start | bytes 2162688 | tf_op jit(solution)/shard_map/all_gather | solution.py:134
  172.8 55.4 %copy-start.4 = (bf16[4,32,8,256]{3,2,1,0:T(8,128)(2,1)}, bf16[4,32,8,256]{3,2,1,0:T(8,128)(2,1)S(1)}, u32[]{:S(2)}) copy-start(bf16[4,32,8,256]{3,2,1,0:T(8,128)(2,1)S(1)} %copy.212) | copy-start | bytes 1572868
  178.4 10.0 %all-to-all-start.3 = ((bf16[32,2,512]{2,1,0:T(2,128)(2,1)}), bf16[32,2,512]{2,1,0:T(2,128)(2,1)S(1)}, u32[]{:S(2)}, u32[]{:S(2)}) async-start(bf16[32,2,512]{2,1,0:T(2,128)(2,1)} %reshape.176), calls=%async_computation.3 | async-start | bytes 131072 | tf_op jit(solution)/shard_map/all_to_all | solution.py:128
  188.8 46.2 %copy-start.1 = (bf16[1024,128]{1,0:T(8,128)(2,1)S(1)}, bf16[1024,128]{1,0:T(8,128)(2,1)}, u32[]{:S(2)}) copy-start(bf16[1024,128]{1,0:T(8,128)(2,1)} %param.35) | copy-start | bytes 786436
  235.1 8.6 %copy-start.2 = (bf16[8,256,128]{2,1,0:T(8,128)(2,1)S(1)}, bf16[8,256,128]{2,1,0:T(8,128)(2,1)}, u32[]{:S(2)}) copy-start(bf16[8,256,128]{2,1,0:T(8,128)(2,1)} %param.20) | copy-start | bytes 1572868
Sparse Core Ops, SparseCore 0:
  12.9 56.3 all-gather.3
  174.2 53.9 all-gather.5
